TPU v7x, 32 devices: a whole 2x2x4 slice. The times are simulated.
32 devices in a mesh: groups: 2 (over y), blk: 16 (over z, x, core).
Axes of the slice: x: 2, y: 2, z: 4, core: 2. Of those that a mesh axis runs over, the one named last changes fastest.
Arguments:
- txt_q: bfloat16 [1024, 1536], P(('groups', 'blk')), parts along dimension 0, may hold values from -40 to 40
- txt_k: bfloat16 [1024, 1536], P(('groups', 'blk')), parts along dimension 0, may hold values from -40 to 40
- txt_v: bfloat16 [1024, 1536], P(('groups', 'blk')), parts along dimension 0, may hold values from -6 to 6
- img_q: bfloat16 [2048, 1536], P(('groups', 'blk')), parts along dimension 0, may hold values from -6 to 6
- img_k: bfloat16 [2048, 1536], P(('groups', 'blk')), parts along dimension 0, may hold values from -6 to 6
- img_v: bfloat16 [2048, 1536], P(('groups', 'blk')), parts along dimension 0, may hold values from -6 to 6
- q_gain: float32 [128], replicated, may hold values from 0.35 to 3.5
- k_gain: float32 [128], replicated, may hold values from 0.35 to 3.5
- places: int32 [2048], P(('groups', 'blk')), parts along dimension 0, may hold values from 0 to 1023, each once
Outputs:
- txt_out: bfloat16 [1024, 1536], P(('groups', 'blk')), parts along dimension 0
- img_out: bfloat16 [2048, 1536], P(('groups', 'blk')), parts along dimension 0
There are 2 independent parts, one for each index of `groups`. A program takes and returns all parts, laid end to end along the dimension named above; an argument that names none is the same for every part. Nothing has to cross between parts.
All inputs are finite; a program needn't handle non-finite values.
Results may differ from a plain program's by a relative error of at most 0.0055.
The roundings to bfloat16 on the way count: a program that leaves them out, or rounds other values in their place, can miss the bound.
Values may be sent and summed in bfloat16 or wider, within the bound.
A program may use at most 64 MiB of HBM per device.

v0:
```python
import jax
import jax.numpy as jnp
from jax import lax
from jax.sharding import PartitionSpec as P

HEADS = 12
HEAD_DIM = 128
GRID_W = 256


rope_theta = 10000.0


def from_partner(block, axis, apart):
    count = lax.axis_size(axis)
    route = []
    for low in range(count):
        high = low | 1 << apart
        if high != low and high < count:
            route += [(low, high), (high, low)]
    return lax.ppermute(block, axis, route)


def passed_along(block, axis, distance):
    devices = range(lax.axis_size(axis))
    route = [((i - distance) % len(devices), i) for i in devices]
    return lax.ppermute(block, axis, route)


def normed(values, gain):
    row_count = values.shape[0]
    heads = values.astype(jnp.float32).reshape(row_count, HEADS, HEAD_DIM)
    mean_sq = jnp.mean(heads * heads, axis=-1, keepdims=True)
    return heads * lax.rsqrt(mean_sq + 1e-06) * gain


def rotate(heads, places):
    row_count = heads.shape[0]
    row_pos = (places // GRID_W).astype(jnp.float32)[:, None]
    col_pos = (places % GRID_W).astype(jnp.float32)[:, None]
    index = jnp.arange(64, dtype=jnp.float32)[None, :]
    freq_row = jnp.exp(-(index - 8.0) / 28.0 * jnp.log(rope_theta))
    freq_col = jnp.exp(-(index - 36.0) / 28.0 * jnp.log(rope_theta))
    angle = jnp.where(
        index < 8.0, 0.0 * row_pos, jnp.where(index < 36.0, row_pos * freq_row, col_pos * freq_col)
    )
    cosine = jnp.cos(angle)[:, None, :]
    sine = jnp.sin(angle)[:, None, :]
    pairs = heads.reshape(row_count, HEADS, 64, 2)
    first = pairs[..., 0]
    second = pairs[..., 1]
    turned = jnp.stack([first * cosine - second * sine, first * sine + second * cosine], axis=-1)
    return turned.reshape(row_count, HEADS, HEAD_DIM)


def update(state_tuple, queries, pair_block):
    running_max, running_sum, running_acc = state_tuple
    key_block = pair_block[0]
    value_block = pair_block[1]
    scores = jnp.einsum("rhd,nhd->rhn", queries, key_block, preferred_element_type=jnp.float32)
    scores = scores / jnp.sqrt(jnp.float32(HEAD_DIM))
    new_max = jnp.maximum(running_max, jnp.max(scores, axis=-1))
    fade_out = jnp.exp(running_max - new_max)
    expo = jnp.exp(scores - new_max[..., None])
    new_sum = running_sum * fade_out + jnp.sum(expo, axis=-1)
    added = jnp.einsum(
        "rhn,nhd->rhd", expo.astype(jnp.bfloat16), value_block, preferred_element_type=jnp.float32
    )
    new_acc = running_acc * fade_out[..., None] + added
    return (new_max, new_sum, new_acc)


def regroup_swap(piece, bit_number):
    return from_partner(piece, "blk", bit_number)


def restore_swap(piece, bit_number):
    return from_partner(piece, "blk", bit_number)


def among_four(stacked, mover):
    index_here = lax.axis_index("blk")
    for bit_number in (0, 1):
        position = 1 - bit_number
        own_bit = index_here >> bit_number & 1
        kept_half = lax.dynamic_index_in_dim(stacked, own_bit, position, keepdims=False)
        sent_half = lax.dynamic_index_in_dim(stacked, 1 - own_bit, position, keepdims=False)
        received = mover(sent_half, bit_number)
        stacked = jnp.where(
            own_bit == 0,
            jnp.stack([kept_half, received], axis=position),
            jnp.stack([received, kept_half], axis=position),
        )
    return stacked


def move_upward(pair_block):
    return passed_along(pair_block, "blk", 4)


def move_downward(pair_block):
    return passed_along(pair_block, "blk", -4)


def per_device(txt_q, txt_k, txt_v, img_q, img_k, img_v, q_gain, k_gain, places):
    txt_count = txt_q.shape[0]
    img_count = img_q.shape[0]
    local_count = txt_count + img_count
    quarter = HEADS // 4
    queries = jnp.concatenate(
        [
            normed(txt_q, q_gain).astype(jnp.bfloat16),
            rotate(normed(img_q, q_gain), places).astype(jnp.bfloat16),
        ],
        axis=0,
    )
    keys_local = jnp.concatenate(
        [
            normed(txt_k, k_gain).astype(jnp.bfloat16),
            rotate(normed(img_k, k_gain), places).astype(jnp.bfloat16),
        ],
        axis=0,
    )
    values_local = jnp.concatenate([txt_v, img_v], axis=0).reshape(local_count, HEADS, HEAD_DIM)
    stacked = jnp.stack([queries, keys_local, values_local], axis=1).reshape(
        local_count, 3, 4, quarter, HEAD_DIM
    )
    stacked = jnp.transpose(stacked, (2, 0, 1, 3, 4)).reshape(
        2, 2, local_count, 3, quarter, HEAD_DIM
    )
    grouped = among_four(stacked, regroup_swap).reshape(4 * local_count, 3, quarter, HEAD_DIM)
    group_q = grouped[:, 0]
    own_pair = jnp.stack([grouped[:, 1], grouped[:, 2]], axis=0)
    group_rows = 4 * local_count
    blocks = lax.axis_size("blk") // 4
    soft_state = (
        jnp.full((group_rows, quarter), -jnp.inf, jnp.float32),
        jnp.zeros((group_rows, quarter), jnp.float32),
        jnp.zeros((group_rows, quarter, HEAD_DIM), jnp.float32),
    )
    soft_state = update(soft_state, group_q, own_pair)
    downward_turns = (blocks - 1) // 2

    def both_turn(turn, loop_state):
        upward, downward, inner = loop_state
        upward = move_upward(upward)
        downward = move_downward(downward)
        inner = update(inner, group_q, upward)
        inner = update(inner, group_q, downward)
        return (upward, downward, inner)

    upward, downward, soft_state = lax.fori_loop(
        0, downward_turns, both_turn, (own_pair, own_pair, soft_state)
    )
    upward = move_upward(upward)
    soft_state = update(soft_state, group_q, upward)
    running_max, running_sum, running_acc = soft_state
    result = (running_acc / running_sum[..., None]).astype(jnp.bfloat16)
    result = result.reshape(2, 2, local_count, quarter, HEAD_DIM)
    returned = among_four(result, restore_swap).reshape(4, local_count, quarter, HEAD_DIM)
    returned = jnp.transpose(returned, (1, 0, 2, 3)).reshape(local_count, HEADS * HEAD_DIM)
    return (returned[:txt_count], returned[txt_count:])


def solution(mesh):
    placed = (
        P(("groups", "blk"), None),
        P(("groups", "blk"), None),
        P(("groups", "blk"), None),
        P(("groups", "blk"), None),
        P(("groups", "blk"), None),
        P(("groups", "blk"), None),
        P(),
        P(),
        P(("groups", "blk")),
    )
    return jax.shard_map(
        per_device,
        mesh=mesh,
        in_specs=placed,
        out_specs=(P(("groups", "blk"), None), P(("groups", "blk"), None)),
        check_vma=False,
    )
```

profile of v0, /device:TPU:0, one launch (start us, length us, event | category | flops | bytes accessed | tf_op | source)
XLA Modules:
  0.0 91.2 jit_solution(9210518236921916494)
XLA Ops:
  0.7 0.7 fusion.45
  1.4 0.7 broadcast_multiply_fusion
  2.1 0.9 convert_multiply_fusion.3
  3.0 1.1 %reshape.405 = f32[32,1,4,3,128]{4,3,2,0,1:T(4,128)S(1)} reshape(bf16[32,1536]{1,0:T(8,128)(2,1)} %param.9) | data formatting | bytes 294912 | tf_op jit(solution)/shard_map/reshape | solution.py:32
  4.0 0.9 convert_multiply_fusion.2
  5.0 1.1 %reshape.407 = f32[32,1,4,3,128]{4,3,2,0,1:T(4,128)S(1)} reshape(bf16[32,1536]{1,0:T(8,128)(2,1)} %param.10) | data formatting | bytes 294912 | tf_op jit(solution)/shard_map/reshape | solution.py:32
  6.1 1.7 %convert_multiply_fusion.1 = f32[64,1536]{1,0:T(8,128)} fusion(bf16[64,1536]{1,0:T(8,128)(2,1)} %param.12), kind=kLoop, calls=%fused_computation.82 | loop fusion | flops 196608 | bytes 589824 | tf_op jit(solution)/shard_map/mul | solution.py:33
  8.0 0.8 convert_multiply_fusion
  10.1 0.3 copy.75
  10.5 0.2 copy.80
  10.8 0.2 copy.105
  11.0 1.1 %mul.322 = f32[64,12,128]{2,1,0:T(8,128)S(1)} reshape(f32[64,1536]{1,0:T(8,128)} %convert_multiply_fusion.1) | data formatting | bytes 786432 | tf_op jit(solution)/shard_map/mul | solution.py:33
  12.4 1.1 %mul.351 = f32[64,12,128]{2,1,0:T(8,128)S(1)} reshape(f32[64,1536]{1,0:T(8,128)} %convert_multiply_fusion) | data formatting | bytes 786432 | tf_op jit(solution)/shard_map/mul | solution.py:33
  13.8 0.9 %multiply_multiply_fusion = (f32[64,12,64,2]{0,3,2,1:T(2,128)S(1)}, f32[64,12,64,2]{0,3,2,1:T(2,128)S(1)}) fusion(f32[64,12,64,2]{0,3,2,1:T(2,128)S(1)} %bitcast.157, f32[64,2]{1,0:T(8,128)S(1)} %mul.354, f32[64,12]{0,1:T(8,128)S(1)} %add_rsqrt_fusion, f32[64,2]{1,0:T(8,128)S(1)} %mul.325, f32[64,12,64,2]{0,3,2,1:T(2,128)S(1)} %bitcast.156, ...), kind=kLoop, calls=%fused_computation.44 | loop fusion | flops 393216 | bytes 1580032 | tf_op jit(solution)/shard_map/mul | solution.py:34
  14.7 0.2 fusion.44
  15.0 2.1 %subtract_convert_fusion.1 = (bf16[64,12,64,1]{0,3,2,1:T(2,128)(2,1)S(1)}, bf16[64,12,64,1]{0,3,2,1:T(2,128)(2,1)S(1)}, bf16[64,12,64,1]{0,3,2,1:T(2,128)(2,1)S(1)}, bf16[64,12,64,1]{0,3,2,1:T(2,128)(2,1)S(1)}) fusion(f32[64,12,64,2]{0,3,2,1:T(2,128)S(1)} %get-tuple-element.64, f32[64,64]{0,1:T(8,128)S(1)} %get-tuple-element.50, ...), kind=kLoop, calls=%fused_computation.54 | loop fusion | flops 786432 | bytes 1212416 | tf_op jit(solution)/shard_map/convert.2
  17.1 1.0 %pad_maximum_fusion.2 = bf16[64,12,64,2]{0,3,2,1:T(2,128)(2,1)S(1)} fusion(bf16[64,12,64,1]{0,3,2,1:T(2,128)(2,1)S(1)} %get-tuple-element.39, bf16[64,12,64,1]{0,3,2,1:T(2,128)(2,1)S(1)} %get-tuple-element.38), kind=kLoop, calls=%fused_computation.48 | loop fusion | flops 393216 | bytes 393216 | tf_op jit(solution)/shard_map/stack | solution.py:52
  18.1 1.0 %pad_maximum_fusion.3 = bf16[64,12,64,2]{0,3,2,1:T(2,128)(2,1)S(1)} fusion(bf16[64,12,64,1]{0,3,2,1:T(2,128)(2,1)S(1)} %get-tuple-element.46, bf16[64,12,64,1]{0,3,2,1:T(2,128)(2,1)S(1)} %get-tuple-element.47), kind=kLoop, calls=%fused_computation.49 | loop fusion | flops 393216 | bytes 393216 | tf_op jit(solution)/shard_map/stack | solution.py:52
  19.1 0.5 pad_maximum_fusion
  19.8 0.3 copy.83
  20.1 0.5 collective-permute-start
  20.6 0.3 copy.106
  20.9 1.1 %collective-permute-done = bf16[2,96,3,3,128]{4,1,0,3,2:T(8,128)(2,1)S(1)} collective-permute-done((bf16[2,96,3,3,128]{4,1,0,3,2:T(8,128)(2,1)S(1)}, bf16[2,96,3,3,128]{4,1,0,3,2:T(8,128)(2,1)S(1)}, u32[]{:S(2)}, u32[]{:S(2)}) %collective-permute-start) | collective-permute-done | bytes 442400 | tf_op jit(solution)/shard_map/ppermute | solution.py:21
  22.2 2.9 %collective-permute-start.1 = (bf16[2,96,3,3,128]{4,1,0,3,2:T(8,128)(2,1)S(1)}, bf16[2,96,3,3,128]{4,1,0,3,2:T(8,128)(2,1)S(1)}, u32[]{:S(2)}, u32[]{:S(2)}) collective-permute-start(bf16[2,96,3,3,128]{4,1,0,3,2:T(8,128)(2,1)S(1)} %get-tuple-element.37), channel_id=1, source_target_pairs={{0,2},{2,0},{1,3},{3,1},{4,6},{6,4},{5,7},{7,5},{8,10},{10,8},{9,1... | collective-permute-start | bytes 1327112 | tf_op jit(solution)/shard_map/ppermute | solution.py:21
  25.1 10.5 %collective-permute-done.1 = bf16[2,96,3,3,128]{4,1,0,3,2:T(8,128)(2,1)S(1)} collective-permute-done((bf16[2,96,3,3,128]{4,1,0,3,2:T(8,128)(2,1)S(1)}, bf16[2,96,3,3,128]{4,1,0,3,2:T(8,128)(2,1)S(1)}, u32[]{:S(2)}, u32[]{:S(2)}) %collective-permute-start.1) | collective-permute-done | bytes 442400 | tf_op jit(solution)/shard_map/ppermute | solution.py:21
  35.8 1.9 %collective-permute-start.2 = (bf16[2,384,3,128]{3,1,2,0:T(8,128)(2,1)S(1)}, bf16[2,384,3,128]{3,1,2,0:T(8,128)(2,1)S(1)}, u32[]{:S(2)}, u32[]{:S(2)}) collective-permute-start(bf16[2,384,3,128]{3,1,2,0:T(8,128)(2,1)S(1)} %pad_maximum_fusion.1), channel_id=1, source_target_pairs={{12,0},{13,1},{14,2},{15,3},{0,4},{1,5},{2,6},{3,7},{4,8},{5,9},{6... | collective-permute-start | bytes 1769480 | tf_op jit(solution)/shard_map/while/body/eval_jaxpr/ppermute | solution.py:27
  37.7 2.1 %collective-permute-start.3 = (bf16[2,384,3,128]{3,1,2,0:T(8,128)(2,1)S(1)}, bf16[2,384,3,128]{3,1,2,0:T(8,128)(2,1)S(1)}, u32[]{:S(2)}, u32[]{:S(2)}) collective-permute-start(bf16[2,384,3,128]{3,1,2,0:T(8,128)(2,1)S(1)} %pad_maximum_fusion.1), channel_id=1, source_target_pairs={{4,0},{5,1},{6,2},{7,3},{8,4},{9,5},{10,6},{11,7},{12,8},{13,9},{1... | collective-permute-start | bytes 1769480 | tf_op jit(solution)/shard_map/while/body/eval_jaxpr/ppermute | solution.py:27
  39.8 0.4 bitcast_reduce_fusion.3
  40.2 13.8 %collective-permute-done.2 = bf16[2,384,3,128]{3,1,2,0:T(8,128)(2,1)S(1)} collective-permute-done((bf16[2,384,3,128]{3,1,2,0:T(8,128)(2,1)S(1)}, bf16[2,384,3,128]{3,1,2,0:T(8,128)(2,1)S(1)}, u32[]{:S(2)}, u32[]{:S(2)}) %collective-permute-start.2) | collective-permute-done | bytes 589856 | tf_op jit(solution)/shard_map/while/body/eval_jaxpr/ppermute | solution.py:27
  54.0 0.3 fusion.4
  54.3 0.4 bitcast_reduce_fusion.2
  54.7 10.7 %collective-permute-done.3 = bf16[2,384,3,128]{3,1,2,0:T(8,128)(2,1)S(1)} collective-permute-done((bf16[2,384,3,128]{3,1,2,0:T(8,128)(2,1)S(1)}, bf16[2,384,3,128]{3,1,2,0:T(8,128)(2,1)S(1)}, u32[]{:S(2)}, u32[]{:S(2)}) %collective-permute-start.3) | collective-permute-done | bytes 589856 | tf_op jit(solution)/shard_map/while/body/eval_jaxpr/ppermute | solution.py:27
  65.4 0.4 bitcast_reduce_fusion.1
  65.8 12.0 %collective-permute-done.4 = bf16[2,384,3,128]{3,1,2,0:T(8,128)(2,1)S(1)} collective-permute-done((bf16[2,384,3,128]{3,1,2,0:T(8,128)(2,1)S(1)}, bf16[2,384,3,128]{3,1,2,0:T(8,128)(2,1)S(1)}, u32[]{:S(2)}, u32[]{:S(2)}) %collective-permute-start.4) | collective-permute-done | bytes 589856 | tf_op jit(solution)/shard_map/ppermute | solution.py:27
  77.8 0.4 bitcast_reduce_fusion
  78.3 0.3 fusion.10
  78.6 0.3 fusion.8
  78.9 0.3 fusion.6
  79.2 0.5 fusion.19
  79.8 0.5 fusion.17
  80.3 0.5 fusion.15
  80.8 0.5 fusion.20
  81.7 1.4 %collective-permute-done.5 = bf16[2,96,3,128]{3,1,2,0:T(8,128)(2,1)S(1)} collective-permute-done((bf16[2,96,3,128]{3,1,2,0:T(8,128)(2,1)S(1)}, bf16[2,96,3,128]{3,1,2,0:T(8,128)(2,1)S(1)}, u32[]{:S(2)}, u32[]{:S(2)}) %collective-permute-start.5) | collective-permute-done | bytes 147488 | tf_op jit(solution)/shard_map/ppermute | solution.py:21
  83.2 1.6 %collective-permute-start.6 = (bf16[2,96,3,128]{3,1,0,2:T(8,128)(2,1)S(1)}, bf16[2,96,3,128]{3,1,0,2:T(8,128)(2,1)S(1)}, u32[]{:S(2)}, u32[]{:S(2)}) collective-permute-start(bf16[2,96,3,128]{3,1,0,2:T(8,128)(2,1)S(1)} %get-tuple-element.43), channel_id=1, source_target_pairs={{0,2},{2,0},{1,3},{3,1},{4,6},{6,4},{5,7},{7,5},{8,10},{10,8},{9,1... | collective-permute-start | bytes 442376 | tf_op jit(solution)/shard_map/ppermute | solution.py:21
  84.7 4.4 %collective-permute-done.6 = bf16[2,96,3,128]{3,1,0,2:T(8,128)(2,1)S(1)} collective-permute-done((bf16[2,96,3,128]{3,1,0,2:T(8,128)(2,1)S(1)}, bf16[2,96,3,128]{3,1,0,2:T(8,128)(2,1)S(1)}, u32[]{:S(2)}, u32[]{:S(2)}) %collective-permute-start.6) | collective-permute-done | bytes 147488 | tf_op jit(solution)/shard_map/ppermute | solution.py:21
  89.2 0.3 copy.116
  89.6 0.8 slice.71
  90.5 0.7 slice.69
  (56 shorter events, 3.3 us)
Async XLA Ops:
  0.6 7.1 %copy-start = (bf16[64,1536]{1,0:T(8,128)(2,1)S(1)}, bf16[64,1536]{1,0:T(8,128)(2,1)}, u32[]{:S(2)}) copy-start(bf16[64,1536]{1,0:T(8,128)(2,1)} %param.12) | copy-start | bytes 589828
  0.6 7.3 %copy-start.1 = (bf16[64,1536]{1,0:T(8,128)(2,1)S(1)}, bf16[64,1536]{1,0:T(8,128)(2,1)}, u32[]{:S(2)}) copy-start(bf16[64,1536]{1,0:T(8,128)(2,1)} %param.13) | copy-start | bytes 589828
  5.0 3.9 %copy-start.5 = (f32[128]{0:T(128)S(1)}, f32[128]{0:T(128)}, u32[]{:S(2)}) copy-start(f32[128]{0:T(128)} %param.15) | copy-start | bytes 1540
  5.0 4.1 %copy-start.4 = (f32[128]{0:T(128)S(1)}, f32[128]{0:T(128)}, u32[]{:S(2)}) copy-start(f32[128]{0:T(128)} %param.16) | copy-start | bytes 1540
  9.1 1.7 %copy-start.2 = (bf16[64,1536]{1,0:T(8,128)(2,1)S(1)}, bf16[64,1536]{1,0:T(8,128)(2,1)}, u32[]{:S(2)}) copy-start(bf16[64,1536]{1,0:T(8,128)(2,1)} %param.14) | copy-start | bytes 589828
  9.1 1.7 %copy-start.3 = (bf16[32,1536]{1,0:T(8,128)(2,1)S(1)}, bf16[32,1536]{1,0:T(8,128)(2,1)}, u32[]{:S(2)}) copy-start(bf16[32,1536]{1,0:T(8,128)(2,1)} %param.11) | copy-start | bytes 294916
  20.1 1.9 %collective-permute-start = (bf16[2,96,3,3,128]{4,1,0,3,2:T(8,128)(2,1)S(1)}, bf16[2,96,3,3,128]{4,1,0,3,2:T(8,128)(2,1)S(1)}, u32[]{:S(2)}, u32[]{:S(2)}) collective-permute-start(bf16[2,96,3,3,128]{4,1,0,3,2:T(8,128)(2,1)S(1)} %bitcast.165), channel_id=1, source_target_pairs={{0,1},{1,0},{2,3},{3,2},{4,5},{5,4},{6,7},{7,6},{8,9},{9,8},{10,11... | collective-permute-start | bytes 1327112 | tf_op jit(solution)/shard_map/ppermute | solution.py:21
  22.2 13.4 %collective-permute-start.1 = (bf16[2,96,3,3,128]{4,1,0,3,2:T(8,128)(2,1)S(1)}, bf16[2,96,3,3,128]{4,1,0,3,2:T(8,128)(2,1)S(1)}, u32[]{:S(2)}, u32[]{:S(2)}) collective-permute-start(bf16[2,96,3,3,128]{4,1,0,3,2:T(8,128)(2,1)S(1)} %get-tuple-element.37), channel_id=1, source_target_pairs={{0,2},{2,0},{1,3},{3,1},{4,6},{6,4},{5,7},{7,5},{8,10},{10,8},{9,1... | collective-permute-start | bytes 1327112 | tf_op jit(solution)/shard_map/ppermute | solution.py:21
  35.8 18.2 %collective-permute-start.2 = (bf16[2,384,3,128]{3,1,2,0:T(8,128)(2,1)S(1)}, bf16[2,384,3,128]{3,1,2,0:T(8,128)(2,1)S(1)}, u32[]{:S(2)}, u32[]{:S(2)}) collective-permute-start(bf16[2,384,3,128]{3,1,2,0:T(8,128)(2,1)S(1)} %pad_maximum_fusion.1), channel_id=1, source_target_pairs={{12,0},{13,1},{14,2},{15,3},{0,4},{1,5},{2,6},{3,7},{4,8},{5,9},{6... | collective-permute-start | bytes 1769480 | tf_op jit(solution)/shard_map/while/body/eval_jaxpr/ppermute | solution.py:27
  37.7 27.7 %collective-permute-start.3 = (bf16[2,384,3,128]{3,1,2,0:T(8,128)(2,1)S(1)}, bf16[2,384,3,128]{3,1,2,0:T(8,128)(2,1)S(1)}, u32[]{:S(2)}, u32[]{:S(2)}) collective-permute-start(bf16[2,384,3,128]{3,1,2,0:T(8,128)(2,1)S(1)} %pad_maximum_fusion.1), channel_id=1, source_target_pairs={{4,0},{5,1},{6,2},{7,3},{8,4},{9,5},{10,6},{11,7},{12,8},{13,9},{1... | collective-permute-start | bytes 1769480 | tf_op jit(solution)/shard_map/while/body/eval_jaxpr/ppermute | solution.py:27
  54.0 23.9 %collective-permute-start.4 = (bf16[2,384,3,128]{3,1,2,0:T(8,128)(2,1)S(1)}, bf16[2,384,3,128]{3,1,2,0:T(8,128)(2,1)S(1)}, u32[]{:S(2)}, u32[]{:S(2)}) collective-permute-start(bf16[2,384,3,128]{3,1,2,0:T(8,128)(2,1)S(1)} %collective-permute-done.2), channel_id=1, source_target_pairs={{12,0},{13,1},{14,2},{15,3},{0,4},{1,5},{2,6},{3,7},{4,8},{5,9},{6... | collective-permute-start | bytes 1769480 | tf_op jit(solution)/shard_map/ppermute | solution.py:27
  81.6 1.4 %collective-permute-start.5 = (bf16[2,96,3,128]{3,1,2,0:T(8,128)(2,1)S(1)}, bf16[2,96,3,128]{3,1,2,0:T(8,128)(2,1)S(1)}, u32[]{:S(2)}, u32[]{:S(2)}) collective-permute-start(bf16[2,96,3,128]{3,1,2,0:T(8,128)(2,1)S(1)} %bitcast.168), channel_id=1, source_target_pairs={{0,1},{1,0},{2,3},{3,2},{4,5},{5,4},{6,7},{7,6},{8,9},{9,8},{10,11... | collective-permute-start | bytes 442376 | tf_op jit(solution)/shard_map/ppermute | solution.py:21
  83.2 6.0 %collective-permute-start.6 = (bf16[2,96,3,128]{3,1,0,2:T(8,128)(2,1)S(1)}, bf16[2,96,3,128]{3,1,0,2:T(8,128)(2,1)S(1)}, u32[]{:S(2)}, u32[]{:S(2)}) collective-permute-start(bf16[2,96,3,128]{3,1,0,2:T(8,128)(2,1)S(1)} %get-tuple-element.43), channel_id=1, source_target_pairs={{0,2},{2,0},{1,3},{3,1},{4,6},{6,4},{5,7},{7,5},{8,10},{10,8},{9,1... | collective-permute-start | bytes 442376 | tf_op jit(solution)/shard_map/ppermute | solution.py:21
where the time goes:
time: 91.6 us; the launch traced here: 91.2 us
  waiting for transfers between devices  53.8 us (59%)
  other arithmetic  14.2 us (16%)
  local copies, waits for them, and re-layouts  9.22 us (10%)
  starting transfers between devices  9.05 us (10%)
  matrix products  3.79 us (4%)
  between operations  1.1 us (1%)
    ppermute x3, waiting for transfers between devices, passed_along(): return lax.ppermute(block, axis, route)  36.5 us
    ppermute x4, waiting for transfers between devices, from_partner(): return lax.ppermute(block, axis, route)  17.4 us
    ppermute x4, starting transfers between devices, from_partner(): return lax.ppermute(block, axis, route)  5.07 us
    mul x4, other arithmetic, normed(): mean_sq = jnp.mean(heads * heads, axis=-1, keepdims=True)  4.29 us
    ppermute x3, starting transfers between devices, passed_along(): return lax.ppermute(block, axis, route)  3.97 us
    mul x4, local copies, waits for them, and re-layouts, normed(): mean_sq = jnp.mean(heads * heads, axis=-1, keepdims=True)  2.23 us
    reshape x2, local copies, waits for them, and re-layouts, normed(): heads = values.astype(jnp.float32).reshape(row_count, HEADS, HEAD_DIM)  2.14 us
    dot_general x4, matrix products, update(): jnp.einsum('rhn,nhd->rhd', expo.astype(jnp.bfloat16), value_block, prefer...  2.11 us
  transfers between devices with their start and end apart: 7, of which 7 were waited for; matrix products, arithmetic and copies ran while one was open for 2% of the time, Pallas kernels for 0%

commit v1 on v0

--- a/solution.py
+++ b/solution.py
@@ -1,6 +1,11 @@
+import functools
+import math
+
 import jax
 import jax.numpy as jnp
 from jax import lax
+from jax.experimental import pallas as pl
+from jax.experimental.pallas import tpu as pltpu
 from jax.sharding import PartitionSpec as P
 
 HEADS = 12
@@ -162,6 +167,237 @@
     return (returned[:txt_count], returned[txt_count:])
 
 
+MESH = pl.DeviceIdType.MESH
+COLUMN = 4
+
+
+def angles(places):
+    row_pos = (places // GRID_W).astype(jnp.float32)[:, None]
+    col_pos = (places % GRID_W).astype(jnp.float32)[:, None]
+    lane = lax.broadcasted_iota(jnp.int32, (1, HEAD_DIM), 1)
+    index = (lane // 2).astype(jnp.float32)
+    freq_row = jnp.exp(-(index - 8.0) / 28.0 * jnp.log(rope_theta))
+    freq_col = jnp.exp(-(index - 36.0) / 28.0 * jnp.log(rope_theta))
+    angle = jnp.where(
+        index < 8.0, 0.0 * row_pos, jnp.where(index < 36.0, row_pos * freq_row, col_pos * freq_col)
+    )
+    sine = jnp.sin(angle)
+    return jnp.cos(angle), jnp.where(lane % 2 == 0, -sine, sine)
+
+
+def attention_kernel(
+    layers, own_heads,
+    txt_q, txt_k, txt_v, img_q, img_k, img_v, q_gain, k_gain, cosine, sine,
+    txt_out, img_out,
+    stage, own, from_x, from_core, out_stage, out_all,
+    z_send, z_recv, x_send, x_recv, c_send, c_recv, o_send, o_recv,
+):
+    texts = txt_q.shape[0]
+    tokens = texts + img_q.shape[0]
+    rows = layers * tokens
+    me = lax.axis_index("blk")
+    layer = me // COLUMN
+    spot = me % COLUMN
+    x_peer = layer * COLUMN + (spot + 2) % COLUMN
+    core_peer = layer * COLUMN + (spot // 2) * 2 + (spot + 1) % 2
+
+    def at_layer(apart):
+        return (layer + apart) % layers
+
+    barrier = pltpu.get_barrier_semaphore()
+    peers = [at_layer(apart) * COLUMN + spot for apart in range(1, layers)] + [x_peer, core_peer]
+    for peer in peers:
+        pl.semaphore_signal(barrier, inc=1, device_id={"blk": peer}, device_id_type=MESH)
+
+    even = lax.broadcasted_iota(jnp.int32, (1, HEAD_DIM), 1) % 2 == 0
+
+    def norm(ref, columns, gain):
+        x = ref[:, columns].astype(jnp.float32)
+        mean_sq = jnp.mean(x * x, axis=-1, keepdims=True)
+        return x * lax.rsqrt(mean_sq + 1e-06) * gain[...]
+
+    def turn(y):
+        other = jnp.where(even, pltpu.roll(y, HEAD_DIM - 1, 1), pltpu.roll(y, 1, 1))
+        return (y * cosine[...] + other * sine[...]).astype(jnp.bfloat16)
+
+    def prepare(head, to, *where):
+        columns = pl.ds(pl.multiple_of(head * HEAD_DIM, HEAD_DIM), HEAD_DIM)
+
+        def put(kind, first, second):
+            to[(where[0], kind, where[1], pl.ds(0, texts))] = first
+            to[(where[0], kind, where[1], pl.ds(texts, tokens - texts))] = second
+
+        put(0, norm(txt_q, columns, q_gain).astype(jnp.bfloat16), turn(norm(img_q, columns, q_gain)))
+        put(1, norm(txt_k, columns, k_gain).astype(jnp.bfloat16), turn(norm(img_k, columns, k_gain)))
+        put(2, txt_v[:, columns], img_v[:, columns])
+
+    order = [layers // 2] + [a for a in range(1, layers) if a != layers // 2]
+
+    def z_copy(i, apart):
+        to = at_layer(apart)
+        return pltpu.make_async_remote_copy(
+            src_ref=stage.at[i, :, apart], dst_ref=own.at[i, :, layer],
+            send_sem=z_send.at[i, apart], recv_sem=z_recv.at[i, layer],
+            device_id={"blk": to * COLUMN + spot}, device_id_type=MESH,
+        )
+
+    def z_arrival(i, apart):
+        source = at_layer(layers - apart)
+        return pltpu.make_async_remote_copy(
+            src_ref=stage.at[i, :, apart], dst_ref=own.at[i, :, source],
+            send_sem=z_send.at[i, apart], recv_sem=z_recv.at[i, source],
+            device_id={"blk": at_layer(apart) * COLUMN + spot}, device_id_type=MESH,
+        )
+
+    def x_copy(i, source):
+        return pltpu.make_async_remote_copy(
+            src_ref=own.at[i, pl.ds(1, 2), source], dst_ref=from_x.at[i, :, source],
+            send_sem=x_send.at[i, source], recv_sem=x_recv.at[i, source],
+            device_id={"blk": x_peer}, device_id_type=MESH,
+        )
+
+    def core_copy(i, which):
+        src = own.at[i, pl.ds(1, 2)] if which == 0 else from_x.at[i]
+        return pltpu.make_async_remote_copy(
+            src_ref=src, dst_ref=from_core.at[i, which],
+            send_sem=c_send.at[i, which], recv_sem=c_recv.at[i, which],
+            device_id={"blk": core_peer}, device_id_type=MESH,
+        )
+
+    def out_copy(i, apart):
+        to = at_layer(apart)
+        head = layer * own_heads + i
+        return pltpu.make_async_remote_copy(
+            src_ref=out_stage.at[i, to], dst_ref=out_all.at[head],
+            send_sem=o_send.at[i, apart], recv_sem=o_recv.at[head],
+            device_id={"blk": to * COLUMN + spot}, device_id_type=MESH,
+        )
+
+    def out_arrival(i, apart):
+        head = at_layer(apart) * own_heads + i
+        return pltpu.make_async_remote_copy(
+            src_ref=out_stage.at[i, layer], dst_ref=out_all.at[head],
+            send_sem=o_send.at[i, apart], recv_sem=o_recv.at[head],
+            device_id={"blk": at_layer(apart) * COLUMN + spot}, device_id_type=MESH,
+        )
+
+    prepare(at_layer(order[0]) * own_heads, stage, 0, order[0])
+    pl.semaphore_wait(barrier, len(peers))
+    z_copy(0, order[0]).start()
+    for i in range(own_heads):
+        for apart in order:
+            if i or apart != order[0]:
+                prepare(at_layer(apart) * own_heads + i, stage, i, apart)
+                z_copy(i, apart).start()
+        prepare(layer * own_heads + i, own, i, layer)
+        x_copy(i, layer).start()
+
+    factor = math.log2(math.e) / math.sqrt(HEAD_DIM)
+
+    @pl.loop(0, own_heads)
+    def _(i):
+        for apart in order:
+            z_arrival(i, apart).wait_recv()
+            x_copy(i, at_layer(layers - apart)).start()
+        core_copy(i, 0).start()
+        queries = own[i, 0].reshape(rows, HEAD_DIM)
+
+        def block(state, keys, values):
+            scores = lax.dot_general(
+                queries, keys.reshape(rows, HEAD_DIM), (((1,), (1,)), ((), ())),
+                preferred_element_type=jnp.float32,
+            ) * factor
+            top = jnp.max(scores, axis=-1, keepdims=True)
+            if state is not None:
+                top = jnp.maximum(top, state[0])
+            expo = jnp.exp2(scores - top)
+            total = jnp.sum(expo, axis=-1, keepdims=True)
+            mixed = jnp.dot(
+                expo.astype(jnp.bfloat16), values.reshape(rows, HEAD_DIM),
+                preferred_element_type=jnp.float32,
+            )
+            if state is not None:
+                fade = jnp.exp2(state[0] - top)
+                total = total + state[1] * fade
+                mixed = mixed + state[2] * fade
+            return top, total, mixed
+
+        state = block(None, own[i, 1], own[i, 2])
+        for source in range(layers):
+            x_copy(i, source).wait_recv()
+        core_copy(i, 1).start()
+        state = block(state, from_x[i, 0], from_x[i, 1])
+        core_copy(i, 0).wait_recv()
+        state = block(state, from_core[i, 0, 0], from_core[i, 0, 1])
+        core_copy(i, 1).wait_recv()
+        _, total, mixed = block(state, from_core[i, 1, 0], from_core[i, 1, 1])
+        out_stage[i] = (mixed / total).astype(jnp.bfloat16).reshape(layers, tokens, HEAD_DIM)
+        for apart in order:
+            out_copy(i, apart).start()
+        out_all[layer * own_heads + i] = out_stage[i, layer]
+
+    for i in range(own_heads):
+        for apart in order:
+            out_arrival(i, apart).wait_recv()
+    for head in range(layers * own_heads):
+        columns = slice(head * HEAD_DIM, (head + 1) * HEAD_DIM)
+        txt_out[:, columns] = out_all[head, :texts]
+        img_out[:, columns] = out_all[head, texts:]
+
+    @pl.loop(0, own_heads)
+    def _(i):
+        for apart in order:
+            z_copy(i, apart).wait_send()
+            out_copy(i, apart).wait_send()
+        for source in range(layers):
+            x_copy(i, source).wait_send()
+        core_copy(i, 0).wait_send()
+        core_copy(i, 1).wait_send()
+
+
+def per_device_fused(layers, txt_q, txt_k, txt_v, img_q, img_k, img_v, q_gain, k_gain, places):
+    own_heads = HEADS // layers
+    tokens = txt_q.shape[0] + img_q.shape[0]
+    cosine, sine = angles(places)
+    bf16, dma = jnp.bfloat16, pltpu.SemaphoreType.DMA
+    block = (tokens, HEAD_DIM)
+    return pl.pallas_call(
+        functools.partial(attention_kernel, layers, own_heads),
+        out_shape=(
+            jax.ShapeDtypeStruct(txt_q.shape, bf16),
+            jax.ShapeDtypeStruct(img_q.shape, bf16),
+        ),
+        in_specs=[pl.BlockSpec(memory_space=pltpu.VMEM)] * 10,
+        out_specs=(pl.BlockSpec(memory_space=pltpu.VMEM),) * 2,
+        scratch_shapes=[
+            pltpu.VMEM((own_heads, 3, layers, *block), bf16),
+            pltpu.VMEM((own_heads, 3, layers, *block), bf16),
+            pltpu.VMEM((own_heads, 2, layers, *block), bf16),
+            pltpu.VMEM((own_heads, 2, 2, layers, *block), bf16),
+            pltpu.VMEM((own_heads, layers, *block), bf16),
+            pltpu.VMEM((HEADS, *block), bf16),
+            dma((own_heads, layers)), dma((own_heads, layers)),
+            dma((own_heads, layers)), dma((own_heads, layers)),
+            dma((own_heads, 2)), dma((own_heads, 2)),
+            dma((own_heads, layers)), dma((HEADS,)),
+        ],
+        compiler_params=pltpu.CompilerParams(
+            collective_id=0, has_side_effects=True, vmem_limit_bytes=40 * 1024 * 1024
+        ),
+    )(
+        txt_q, txt_k, txt_v, img_q, img_k, img_v,
+        q_gain.reshape(1, HEAD_DIM), k_gain.reshape(1, HEAD_DIM), cosine, sine,
+    )
+
+
+def per_device_any(txt_q, txt_k, txt_v, img_q, img_k, img_v, q_gain, k_gain, places):
+    layers, left_over = divmod(lax.axis_size("blk"), COLUMN)
+    whole_tiles = txt_q.shape[0] % 16 == 0 and img_q.shape[0] % 16 == 0
+    fits = left_over == 0 and layers > 1 and HEADS % max(layers, 1) == 0 and whole_tiles
+    part = functools.partial(per_device_fused, layers) if fits else per_device
+    return part(txt_q, txt_k, txt_v, img_q, img_k, img_v, q_gain, k_gain, places)
+
+
 def solution(mesh):
     placed = (
         P(("groups", "blk"), None),
@@ -175,7 +411,7 @@
         P(("groups", "blk")),
     )
     return jax.shard_map(
-        per_device,
+        per_device_any,
         mesh=mesh,
         in_specs=placed,
         out_specs=(P(("groups", "blk"), None), P(("groups", "blk"), None)),

time: 91.6 us -> 51 us (0.56)
  waiting for transfers between devices: 53.8 us -> 0 us
  Pallas kernels: 0 us -> 41.2 us
  other arithmetic: 14.2 us -> 1.6 us
  starting transfers between devices: 9.05 us -> 0 us
  matrix products: 3.79 us -> 0 us
  local copies, waits for them, and re-layouts: 9.22 us -> 7.19 us
    ppermute x7 -> x0, waiting for transfers between devices: 53.8 us -> none  [the longest x3 36.5 us: passed_along(): return lax.ppermute(block, axis, route)]
    pallas_call x0 -> x1, Pallas kernels: none -> 41.2 us  [per_device_fused(): pl.pallas_call(functools.partial(attention_kernel, layers, own_heads), ou...]
    ppermute x7 -> x0, starting transfers between devices: 9.05 us -> none  [the longest x4 5.07 us: from_partner(): return lax.ppermute(block, axis, route)]
    unnamed x13 -> x18, local copies, waits for them, and re-layouts: 0.32 us -> 7.19 us
    mul x6 -> x1, other arithmetic: 5.88 us -> 0.67 us  [angles(): 0.0 * row_pos]
    another operation x5 -> x0, other arithmetic: 4.74 us -> none
    dot_general x8 -> x0, matrix products: 3.79 us -> none  [the longest x4 2.11 us: update(): jnp.einsum('rhn,nhd->rhd', expo.astype(jnp.bfloat16), value_block, prefer...]
    mul x6 -> x0, local copies, waits for them, and re-layouts: 2.49 us -> none  [the longest x4 2.23 us: normed(): mean_sq = jnp.mean(heads * heads, axis=-1, keepdims=True)]
  transfers between devices with their start and end apart: 7 -> 0, of which waited for: 7 -> 0; matrix products, arithmetic and copies ran while one was open for 2% -> 0% of each run, Pallas kernels for 0% -> 0%
where the time goes in v1:
time: 51 us; the launch traced here: 50.7 us
  Pallas kernels  41.2 us (81%)
  local copies, waits for them, and re-layouts  7.19 us (14%)
  other arithmetic  1.6 us (3%)
  between operations  0.68 us (1%)
    pallas_call x1, Pallas kernels, per_device_fused(): pl.pallas_call(functools.partial(attention_kernel, layers, own_heads), ou...  41.2 us
    unnamed x18, local copies, waits for them, and re-layouts  7.19 us

profile of v1, /device:TPU:0, one launch (start us, length us, event | category | flops | bytes accessed | tf_op | source)
XLA Modules:
  0.0 50.7 jit_solution(1641167421529007728)
XLA Ops:
  0.6 0.0 copy-start.3
  0.6 0.7 %fusion.3 = f32[64]{0:T(128)S(1)} fusion(s32[64]{0:T(128)} %param.17), kind=kLoop, calls=%fused_computation.15 | loop fusion | flops 768 | bytes 512 | tf_op jit(solution)/shard_map/convert_element_type | solution.py:176
  1.3 0.7 %broadcast_multiply_fusion = (f32[64]{0:T(128)S(1)}, f32[64]{0:T(128)S(1)}) fusion(s32[64]{0:T(128)} %param.17), kind=kLoop, calls=%fused_computation.20 | loop fusion | flops 1088 | bytes 768 | tf_op jit(solution)/shard_map/mul | solution.py:182
  2.0 0.2 negate_select_fusion
  2.3 0.0 copy-done.3
  2.3 0.0 copy-start
  2.3 0.9 %copy-done = bf16[64,1536]{1,0:T(8,128)(2,1)S(1)} copy-done((bf16[64,1536]{1,0:T(8,128)(2,1)S(1)}, bf16[64,1536]{1,0:T(8,128)(2,1)}, u32[]{:S(2)}) %copy-start) | copy-done | bytes 196632
  3.2 0.0 copy-start.1
  3.2 0.9 %copy-done.1 = bf16[64,1536]{1,0:T(8,128)(2,1)S(1)} copy-done((bf16[64,1536]{1,0:T(8,128)(2,1)S(1)}, bf16[64,1536]{1,0:T(8,128)(2,1)}, u32[]{:S(2)}) %copy-start.1) | copy-done | bytes 196632
  4.1 0.0 copy-start.2
  4.1 0.9 %copy-done.2 = bf16[64,1536]{1,0:T(8,128)(2,1)S(1)} copy-done((bf16[64,1536]{1,0:T(8,128)(2,1)S(1)}, bf16[64,1536]{1,0:T(8,128)(2,1)}, u32[]{:S(2)}) %copy-start.2) | copy-done | bytes 196632
  5.1 0.0 copy-start.4
  5.1 0.9 %copy-done.4 = bf16[32,1536]{1,0:T(8,128)(2,1)S(1)} copy-done((bf16[32,1536]{1,0:T(8,128)(2,1)S(1)}, bf16[32,1536]{1,0:T(8,128)(2,1)}, u32[]{:S(2)}) %copy-start.4) | copy-done | bytes 98328
  5.9 0.0 copy-start.5
  5.9 0.9 %copy-done.5 = bf16[32,1536]{1,0:T(8,128)(2,1)S(1)} copy-done((bf16[32,1536]{1,0:T(8,128)(2,1)S(1)}, bf16[32,1536]{1,0:T(8,128)(2,1)}, u32[]{:S(2)}) %copy-start.5) | copy-done | bytes 98328
  6.8 0.0 copy-start.6
  6.8 0.7 %copy-done.6 = f32[128]{0:T(128)S(1)} copy-done((f32[128]{0:T(128)S(1)}, f32[128]{0:T(128)}, u32[]{:S(2)}) %copy-start.6) | copy-done | bytes 536
  7.5 0.0 copy-start.7
  7.5 0.7 %copy-done.7 = f32[128]{0:T(128)S(1)} copy-done((f32[128]{0:T(128)S(1)}, f32[128]{0:T(128)}, u32[]{:S(2)}) %copy-start.7) | copy-done | bytes 536
  8.1 41.2 %shard_map.104 = (bf16[32,1536]{1,0:T(8,128)(2,1)S(1)}, bf16[64,1536]{1,0:T(8,128)(2,1)S(1)}) custom-call(bf16[32,1536]{1,0:T(8,128)(2,1)S(1)} %copy-done.3, bf16[32,1536]{1,0:T(8,128)(2,1)S(1)} %copy-done.4, bf16[32,1536]{1,0:T(8,128)(2,1)S(1)} %copy-done.5, bf16[64,1536]{1,0:T(8,128)(2,1)S(1)} %copy-done, bf16[64,1536]{1,0:T(8,128)(2,1)S(1)} %copy-done.1, ...), custom_call_target="tpu_custom_call" | custom-call | tf_op jit(solution)/shard_map/pallas_call | solution.py:364
  49.4 0.6 %copy.13 = bf16[32,1536]{1,0:T(8,128)(2,1)} copy(bf16[32,1536]{1,0:T(8,128)(2,1)S(1)} %get-tuple-element.12) | data formatting | bytes 196608
  50.0 0.7 %copy.14 = bf16[64,1536]{1,0:T(8,128)(2,1)} copy(bf16[64,1536]{1,0:T(8,128)(2,1)S(1)} %get-tuple-element.13) | data formatting | bytes 393216
  (3 shorter events, 0.0 us)
Async XLA Ops:
  0.6 1.6 %copy-start.3 = (bf16[32,1536]{1,0:T(8,128)(2,1)S(1)}, bf16[32,1536]{1,0:T(8,128)(2,1)}, u32[]{:S(2)}) copy-start(bf16[32,1536]{1,0:T(8,128)(2,1)} %txt_q.1) | copy-start | bytes 294916
  2.3 0.9 %copy-start = (bf16[64,1536]{1,0:T(8,128)(2,1)S(1)}, bf16[64,1536]{1,0:T(8,128)(2,1)}, u32[]{:S(2)}) copy-start(bf16[64,1536]{1,0:T(8,128)(2,1)} %img_q.1) | copy-start | bytes 589828
  3.2 0.9 %copy-start.1 = (bf16[64,1536]{1,0:T(8,128)(2,1)S(1)}, bf16[64,1536]{1,0:T(8,128)(2,1)}, u32[]{:S(2)}) copy-start(bf16[64,1536]{1,0:T(8,128)(2,1)} %img_k.1) | copy-start | bytes 589828
  4.1 0.9 %copy-start.2 = (bf16[64,1536]{1,0:T(8,128)(2,1)S(1)}, bf16[64,1536]{1,0:T(8,128)(2,1)}, u32[]{:S(2)}) copy-start(bf16[64,1536]{1,0:T(8,128)(2,1)} %img_v.1) | copy-start | bytes 589828
  5.1 0.9 %copy-start.4 = (bf16[32,1536]{1,0:T(8,128)(2,1)S(1)}, bf16[32,1536]{1,0:T(8,128)(2,1)}, u32[]{:S(2)}) copy-start(bf16[32,1536]{1,0:T(8,128)(2,1)} %txt_k.1) | copy-start | bytes 294916
  5.9 0.9 %copy-start.5 = (bf16[32,1536]{1,0:T(8,128)(2,1)S(1)}, bf16[32,1536]{1,0:T(8,128)(2,1)}, u32[]{:S(2)}) copy-start(bf16[32,1536]{1,0:T(8,128)(2,1)} %txt_v.1) | copy-start | bytes 294916
  6.8 0.7 %copy-start.6 = (f32[128]{0:T(128)S(1)}, f32[128]{0:T(128)}, u32[]{:S(2)}) copy-start(f32[128]{0:T(128)} %param.15) | copy-start | bytes 1540
  7.5 0.7 %copy-start.7 = (f32[128]{0:T(128)S(1)}, f32[128]{0:T(128)}, u32[]{:S(2)}) copy-start(f32[128]{0:T(128)} %param.16) | copy-start | bytes 1540

commit v2 on v1

--- a/solution.py
+++ b/solution.py
@@ -172,12 +172,17 @@
 
 
 def angles(places):
-    row_pos = (places // GRID_W).astype(jnp.float32)[:, None]
-    col_pos = (places % GRID_W).astype(jnp.float32)[:, None]
+    count = places.shape[1]
+    square = (count, count)
+    diagonal = lax.broadcasted_iota(jnp.int32, square, 0) == lax.broadcasted_iota(jnp.int32, square, 1)
+    spread = jnp.broadcast_to(places.astype(jnp.float32), square)
+    token = jnp.sum(jnp.where(diagonal, spread, 0.0), axis=1, keepdims=True).astype(jnp.int32)
+    row_pos = (token // GRID_W).astype(jnp.float32)
+    col_pos = (token % GRID_W).astype(jnp.float32)
     lane = lax.broadcasted_iota(jnp.int32, (1, HEAD_DIM), 1)
     index = (lane // 2).astype(jnp.float32)
-    freq_row = jnp.exp(-(index - 8.0) / 28.0 * jnp.log(rope_theta))
-    freq_col = jnp.exp(-(index - 36.0) / 28.0 * jnp.log(rope_theta))
+    freq_row = jnp.exp(-(index - 8.0) / 28.0 * math.log(rope_theta))
+    freq_col = jnp.exp(-(index - 36.0) / 28.0 * math.log(rope_theta))
     angle = jnp.where(
         index < 8.0, 0.0 * row_pos, jnp.where(index < 36.0, row_pos * freq_row, col_pos * freq_col)
     )
@@ -187,10 +192,12 @@
 
 def attention_kernel(
     layers, own_heads,
-    txt_q, txt_k, txt_v, img_q, img_k, img_v, q_gain, k_gain, cosine, sine,
+    txt_q_in, txt_k_in, txt_v_in, img_q_in, img_k_in, img_v_in, q_gain_in, k_gain_in, places_in,
     txt_out, img_out,
+    txt_q, txt_k, txt_v, img_q, img_k, img_v, q_gain, k_gain, places,
+    cosine, sine, load_sem,
     stage, own, from_x, from_core, out_stage, out_all,
-    z_send, z_recv, x_send, x_recv, c_send, c_recv, o_send, o_recv,
+    z_send, z_recv, q_send, q_recv, x_send, x_recv, c_send, c_recv, o_send, o_recv,
 ):
     texts = txt_q.shape[0]
     tokens = texts + img_q.shape[0]
@@ -201,6 +208,17 @@
     x_peer = layer * COLUMN + (spot + 2) % COLUMN
     core_peer = layer * COLUMN + (spot // 2) * 2 + (spot + 1) % 2
 
+    loads = [
+        pltpu.make_async_copy(source, to, load_sem.at[n])
+        for n, (source, to) in enumerate((
+            (places_in, places), (q_gain_in, q_gain), (k_gain_in, k_gain),
+            (txt_q_in, txt_q), (img_q_in, img_q), (txt_k_in, txt_k),
+            (img_k_in, img_k), (txt_v_in, txt_v), (img_v_in, img_v),
+        ))
+    ]
+    for load in loads:
+        load.start()
+
     def at_layer(apart):
         return (layer + apart) % layers
 
@@ -220,32 +238,39 @@
         other = jnp.where(even, pltpu.roll(y, HEAD_DIM - 1, 1), pltpu.roll(y, 1, 1))
         return (y * cosine[...] + other * sine[...]).astype(jnp.bfloat16)
 
-    def prepare(head, to, *where):
-        columns = pl.ds(pl.multiple_of(head * HEAD_DIM, HEAD_DIM), HEAD_DIM)
-
-        def put(kind, first, second):
-            to[(where[0], kind, where[1], pl.ds(0, texts))] = first
-            to[(where[0], kind, where[1], pl.ds(texts, tokens - texts))] = second
-
-        put(0, norm(txt_q, columns, q_gain).astype(jnp.bfloat16), turn(norm(img_q, columns, q_gain)))
-        put(1, norm(txt_k, columns, k_gain).astype(jnp.bfloat16), turn(norm(img_k, columns, k_gain)))
-        put(2, txt_v[:, columns], img_v[:, columns])
+    def columns_of(head):
+        return pl.ds(pl.multiple_of(head * HEAD_DIM, HEAD_DIM), HEAD_DIM)
+
+    def put(to, i, kind, slot, first, second):
+        to[i, kind, slot, pl.ds(0, texts)] = first
+        to[i, kind, slot, pl.ds(texts, tokens - texts)] = second
+
+    def prepare_pair(head, to, i, slot):
+        columns = columns_of(head)
+        put(to, i, 1, slot, norm(txt_k, columns, k_gain).astype(jnp.bfloat16), turn(norm(img_k, columns, k_gain)))
+        put(to, i, 2, slot, txt_v[:, columns], img_v[:, columns])
+
+    def prepare_queries(head, to, i, slot):
+        columns = columns_of(head)
+        put(to, i, 0, slot, norm(txt_q, columns, q_gain).astype(jnp.bfloat16), turn(norm(img_q, columns, q_gain)))
 
     order = [layers // 2] + [a for a in range(1, layers) if a != layers // 2]
-
-    def z_copy(i, apart):
-        to = at_layer(apart)
-        return pltpu.make_async_remote_copy(
-            src_ref=stage.at[i, :, apart], dst_ref=own.at[i, :, layer],
-            send_sem=z_send.at[i, apart], recv_sem=z_recv.at[i, layer],
-            device_id={"blk": to * COLUMN + spot}, device_id_type=MESH,
-        )
-
-    def z_arrival(i, apart):
+    PAIR, QUERY = (pl.ds(1, 2), z_send, z_recv), (pl.ds(0, 1), q_send, q_recv)
+
+    def z_copy(what, i, apart):
+        kinds, send, recv = what
+        return pltpu.make_async_remote_copy(
+            src_ref=stage.at[i, kinds, apart], dst_ref=own.at[i, kinds, layer],
+            send_sem=send.at[i, apart], recv_sem=recv.at[i, layer],
+            device_id={"blk": at_layer(apart) * COLUMN + spot}, device_id_type=MESH,
+        )
+
+    def z_arrival(what, i, apart):
+        kinds, send, recv = what
         source = at_layer(layers - apart)
         return pltpu.make_async_remote_copy(
-            src_ref=stage.at[i, :, apart], dst_ref=own.at[i, :, source],
-            send_sem=z_send.at[i, apart], recv_sem=z_recv.at[i, source],
+            src_ref=stage.at[i, kinds, apart], dst_ref=own.at[i, kinds, source],
+            send_sem=send.at[i, apart], recv_sem=recv.at[i, source],
             device_id={"blk": at_layer(apart) * COLUMN + spot}, device_id_type=MESH,
         )
 
@@ -281,25 +306,53 @@
             device_id={"blk": at_layer(apart) * COLUMN + spot}, device_id_type=MESH,
         )
 
-    prepare(at_layer(order[0]) * own_heads, stage, 0, order[0])
-    pl.semaphore_wait(barrier, len(peers))
-    z_copy(0, order[0]).start()
-    for i in range(own_heads):
-        for apart in order:
-            if i or apart != order[0]:
-                prepare(at_layer(apart) * own_heads + i, stage, i, apart)
-                z_copy(i, apart).start()
-        prepare(layer * own_heads + i, own, i, layer)
+    loads[0].wait()
+    cosine[...], sine[...] = angles(places[...])
+    for load in loads[1:]:
+        load.wait()
+    window = 2
+    units = [(PAIR, i) for i in range(own_heads)] + [(QUERY, i) for i in range(own_heads)]
+
+    def go_on(n, apart):
+        z_copy(*units[n], apart).wait_send()
+        if n + window < len(units):
+            z_copy(*units[n + window], apart).start()
+
+    for i in range(own_heads):
+        for apart in order:
+            prepare_pair(at_layer(apart) * own_heads + i, stage, i, apart)
+            if i == 0 and apart == order[0]:
+                pl.semaphore_wait(barrier, len(peers))
+            if i < window:
+                z_copy(PAIR, i, apart).start()
+        prepare_pair(layer * own_heads + i, own, i, layer)
         x_copy(i, layer).start()
+    for i in range(own_heads):
+        for apart in order:
+            prepare_queries(at_layer(apart) * own_heads + i, stage, i, apart)
+        prepare_queries(layer * own_heads + i, own, i, layer)
+
+    def relay(i):
+        for source in range(layers):
+            x_copy(i, source).wait_recv()
+        core_copy(i, 1).start()
+
+    for i in range(own_heads):
+        for apart in order:
+            z_arrival(PAIR, i, apart).wait_recv()
+            x_copy(i, at_layer(layers - apart)).start()
+            go_on(i, apart)
+        core_copy(i, 0).start()
+        if i:
+            relay(i - 1)
+    relay(own_heads - 1)
 
     factor = math.log2(math.e) / math.sqrt(HEAD_DIM)
 
-    @pl.loop(0, own_heads)
-    def _(i):
-        for apart in order:
-            z_arrival(i, apart).wait_recv()
-            x_copy(i, at_layer(layers - apart)).start()
-        core_copy(i, 0).start()
+    def step(i):
+        for apart in order:
+            z_arrival(QUERY, i, apart).wait_recv()
+            go_on(own_heads + i, apart)
         queries = own[i, 0].reshape(rows, HEAD_DIM)
 
         def block(state, keys, values):
@@ -323,9 +376,6 @@
             return top, total, mixed
 
         state = block(None, own[i, 1], own[i, 2])
-        for source in range(layers):
-            x_copy(i, source).wait_recv()
-        core_copy(i, 1).start()
         state = block(state, from_x[i, 0], from_x[i, 1])
         core_copy(i, 0).wait_recv()
         state = block(state, from_core[i, 0, 0], from_core[i, 0, 1])
@@ -337,6 +387,9 @@
         out_all[layer * own_heads + i] = out_stage[i, layer]
 
     for i in range(own_heads):
+        step(i)
+
+    for i in range(own_heads):
         for apart in order:
             out_arrival(i, apart).wait_recv()
     for head in range(layers * own_heads):
@@ -344,10 +397,8 @@
         txt_out[:, columns] = out_all[head, :texts]
         img_out[:, columns] = out_all[head, texts:]
 
-    @pl.loop(0, own_heads)
-    def _(i):
-        for apart in order:
-            z_copy(i, apart).wait_send()
+    for i in range(own_heads):
+        for apart in order:
             out_copy(i, apart).wait_send()
         for source in range(layers):
             x_copy(i, source).wait_send()
@@ -358,7 +409,6 @@
 def per_device_fused(layers, txt_q, txt_k, txt_v, img_q, img_k, img_v, q_gain, k_gain, places):
     own_heads = HEADS // layers
     tokens = txt_q.shape[0] + img_q.shape[0]
-    cosine, sine = angles(places)
     bf16, dma = jnp.bfloat16, pltpu.SemaphoreType.DMA
     block = (tokens, HEAD_DIM)
     return pl.pallas_call(
@@ -367,9 +417,16 @@
             jax.ShapeDtypeStruct(txt_q.shape, bf16),
             jax.ShapeDtypeStruct(img_q.shape, bf16),
         ),
-        in_specs=[pl.BlockSpec(memory_space=pltpu.VMEM)] * 10,
+        in_specs=[pl.BlockSpec(memory_space=pltpu.HBM)] * 9,
         out_specs=(pl.BlockSpec(memory_space=pltpu.VMEM),) * 2,
         scratch_shapes=[
+            *[pltpu.VMEM(x.shape, bf16) for x in (txt_q, txt_k, txt_v, img_q, img_k, img_v)],
+            pltpu.VMEM((1, HEAD_DIM), jnp.float32),
+            pltpu.VMEM((1, HEAD_DIM), jnp.float32),
+            pltpu.VMEM((1, places.shape[0]), jnp.int32),
+            pltpu.VMEM((img_q.shape[0], HEAD_DIM), jnp.float32),
+            pltpu.VMEM((img_q.shape[0], HEAD_DIM), jnp.float32),
+            dma((9,)),
             pltpu.VMEM((own_heads, 3, layers, *block), bf16),
             pltpu.VMEM((own_heads, 3, layers, *block), bf16),
             pltpu.VMEM((own_heads, 2, layers, *block), bf16),
@@ -378,15 +435,17 @@
             pltpu.VMEM((HEADS, *block), bf16),
             dma((own_heads, layers)), dma((own_heads, layers)),
             dma((own_heads, layers)), dma((own_heads, layers)),
+            dma((own_heads, layers)), dma((own_heads, layers)),
             dma((own_heads, 2)), dma((own_heads, 2)),
             dma((own_heads, layers)), dma((HEADS,)),
         ],
         compiler_params=pltpu.CompilerParams(
-            collective_id=0, has_side_effects=True, vmem_limit_bytes=40 * 1024 * 1024
+            collective_id=0, has_side_effects=True, vmem_limit_bytes=63 * 1024 * 1024
         ),
     )(
         txt_q, txt_k, txt_v, img_q, img_k, img_v,
-        q_gain.reshape(1, HEAD_DIM), k_gain.reshape(1, HEAD_DIM), cosine, sine,
+        q_gain.reshape(1, HEAD_DIM), k_gain.reshape(1, HEAD_DIM),
+        places.reshape(1, -1),
     )
 
 

time: 51 us -> 40.1 us (0.79)
  local copies, waits for them, and re-layouts: 7.19 us -> 2.26 us
  Pallas kernels: 41.2 us -> 37 us
  other arithmetic: 1.6 us -> 0 us
    unnamed x18 -> x4, local copies, waits for them, and re-layouts: 7.19 us -> 2.26 us
    pallas_call x1, Pallas kernels: 41.2 us -> 37 us  [per_device_fused(): pl.pallas_call(functools.partial(attention_kernel, layers, own_heads), ou...]
    convert_element_type x1 -> x0, other arithmetic: 0.7 us -> none  [angles(): col_pos = (places % GRID_W).astype(jnp.float32)[:, None]]
    mul x1 -> x0, other arithmetic: 0.67 us -> none  [angles(): 0.0 * row_pos]
where the time goes in v2:
time: 40.1 us; the launch traced here: 39.9 us
  Pallas kernels  37 us (92%)
  local copies, waits for them, and re-layouts  2.26 us (6%)
  between operations  0.65 us (2%)
    pallas_call x1, Pallas kernels, per_device_fused(): pl.pallas_call(functools.partial(attention_kernel, layers, own_heads), ou...  37 us
    unnamed x4, local copies, waits for them, and re-layouts  2.26 us

profile of v2, /device:TPU:0, one launch (start us, length us, event | category | flops | bytes accessed | tf_op | source)
XLA Modules:
  0.0 39.9 jit_solution(2093534575998414606)
XLA Ops:
  0.6 37.0 %shard_map.104 = (bf16[32,1536]{1,0:T(8,128)(2,1)}, bf16[64,1536]{1,0:T(8,128)(2,1)}) custom-call(bf16[32,1536]{1,0:T(8,128)(2,1)} %txt_q_in.1, bf16[32,1536]{1,0:T(8,128)(2,1)} %txt_k_in.1, bf16[32,1536]{1,0:T(8,128)(2,1)} %txt_v_in.1, bf16[64,1536]{1,0:T(8,128)(2,1)} %img_q_in.1, bf16[64,1536]{1,0:T(8,128)(2,1)} %img_k_in.1, bf16[64,1536]{1,0:T(8,128)(2,1)} %img_v_in.1, ...), custom_call_target="tpu_custom_call" | custom-call | tf_op jit(solution)/shard_map/pallas_call | solution.py:414
  37.6 0.0 copy-start
  37.6 1.6 %copy.13 = bf16[32,1536]{1,0:T(8,128)(2,1)} copy(bf16[32,1536]{1,0:T(8,128)(2,1)} %get-tuple-element.4) | data formatting | bytes 196608
  39.2 0.0 copy-done
  39.2 0.7 %copy.14 = bf16[64,1536]{1,0:T(8,128)(2,1)} copy(bf16[64,1536]{1,0:T(8,128)(2,1)S(1)} %copy-done) | data formatting | bytes 393216
Async XLA Ops:
  37.6 1.6 %copy-start = (bf16[64,1536]{1,0:T(8,128)(2,1)S(1)}, bf16[64,1536]{1,0:T(8,128)(2,1)}, u32[]{:S(2)}) copy-start(bf16[64,1536]{1,0:T(8,128)(2,1)} %get-tuple-element.5) | copy-start | bytes 589828

commit v3 on v2

--- a/solution.py
+++ b/solution.py
@@ -254,7 +254,7 @@
         columns = columns_of(head)
         put(to, i, 0, slot, norm(txt_q, columns, q_gain).astype(jnp.bfloat16), turn(norm(img_q, columns, q_gain)))
 
-    order = [layers // 2] + [a for a in range(1, layers) if a != layers // 2]
+    order = list(range(1, layers))
     PAIR, QUERY = (pl.ds(1, 2), z_send, z_recv), (pl.ds(0, 1), q_send, q_recv)
 
     def z_copy(what, i, apart):
@@ -411,6 +411,9 @@
     tokens = txt_q.shape[0] + img_q.shape[0]
     bf16, dma = jnp.bfloat16, pltpu.SemaphoreType.DMA
     block = (tokens, HEAD_DIM)
+    hold = functools.partial(pltpu.with_memory_space_constraint, memory_space=pltpu.HBM)
+    txt_q, txt_k, txt_v, img_q, img_k, img_v = map(hold, (txt_q, txt_k, txt_v, img_q, img_k, img_v))
+    q_gain, k_gain, places = (hold(x.reshape(1, -1)) for x in (q_gain, k_gain, places))
     return pl.pallas_call(
         functools.partial(attention_kernel, layers, own_heads),
         out_shape=(
@@ -423,7 +426,7 @@
             *[pltpu.VMEM(x.shape, bf16) for x in (txt_q, txt_k, txt_v, img_q, img_k, img_v)],
             pltpu.VMEM((1, HEAD_DIM), jnp.float32),
             pltpu.VMEM((1, HEAD_DIM), jnp.float32),
-            pltpu.VMEM((1, places.shape[0]), jnp.int32),
+            pltpu.VMEM(places.shape, jnp.int32),
             pltpu.VMEM((img_q.shape[0], HEAD_DIM), jnp.float32),
             pltpu.VMEM((img_q.shape[0], HEAD_DIM), jnp.float32),
             dma((9,)),
@@ -440,12 +443,11 @@
             dma((own_heads, layers)), dma((HEADS,)),
         ],
         compiler_params=pltpu.CompilerParams(
-            collective_id=0, has_side_effects=True, vmem_limit_bytes=63 * 1024 * 1024
+            collective_id=0, has_side_effects=True, vmem_limit_bytes=40 * 1024 * 1024
         ),
     )(
         txt_q, txt_k, txt_v, img_q, img_k, img_v,
-        q_gain.reshape(1, HEAD_DIM), k_gain.reshape(1, HEAD_DIM),
-        places.reshape(1, -1),
+        q_gain, k_gain, places,
     )
 
 

time: 40.1 us -> 37.7 us (0.940)
  Pallas kernels: 37 us -> 35.5 us
  local copies, waits for them, and re-layouts: 2.26 us -> 1.32 us
    pallas_call x1, Pallas kernels: 37 us -> 35.5 us  [per_device_fused(): pl.pallas_call(functools.partial(attention_kernel, layers, own_heads), ou...]
    unnamed x4 -> x2, local copies, waits for them, and re-layouts: 2.26 us -> 1.32 us
where the time goes in v3:
time: 37.7 us; the launch traced here: 37.5 us
  Pallas kernels  35.5 us (94%)
  local copies, waits for them, and re-layouts  1.32 us (4%)
  between operations  0.64 us (2%)
    pallas_call x1, Pallas kernels, per_device_fused(): pl.pallas_call(functools.partial(attention_kernel, layers, own_heads), ou...  35.5 us
    unnamed x2, local copies, waits for them, and re-layouts  1.32 us

profile of v3, /device:TPU:0, one launch (start us, length us, event | category | flops | bytes accessed | tf_op | source)
XLA Modules:
  0.0 37.5 jit_solution(2835450071530373025)
XLA Ops:
  0.6 35.5 %shard_map.104 = (bf16[32,1536]{1,0:T(8,128)(2,1)S(1)}, bf16[64,1536]{1,0:T(8,128)(2,1)S(1)}) custom-call(bf16[32,1536]{1,0:T(8,128)(2,1)} %txt_q_in.1, bf16[32,1536]{1,0:T(8,128)(2,1)} %txt_k_in.1, bf16[32,1536]{1,0:T(8,128)(2,1)} %txt_v_in.1, bf16[64,1536]{1,0:T(8,128)(2,1)} %img_q_in.1, bf16[64,1536]{1,0:T(8,128)(2,1)} %img_k_in.1, ...), custom_call_target="tpu_custom_call" | custom-call | tf_op jit(solution)/shard_map/pallas_call | solution.py:417
  36.2 0.6 %copy.13 = bf16[32,1536]{1,0:T(8,128)(2,1)} copy(bf16[32,1536]{1,0:T(8,128)(2,1)S(1)} %get-tuple-element.4) | data formatting | bytes 196608
  36.8 0.7 %copy.14 = bf16[64,1536]{1,0:T(8,128)(2,1)} copy(bf16[64,1536]{1,0:T(8,128)(2,1)S(1)} %get-tuple-element.5) | data formatting | bytes 393216
